TPU v7x, 512 devices: a whole 4x8x8 slice. The times are simulated.
512 devices in a mesh: sib: 2 (over core), row: 16 (over z, y_lo), col: 16 (over x, y_hi).
Axes of the slice: x: 4, y: 8 (y_hi: 4, y_lo: 2; y = y_hi * 2 + y_lo), z: 8, core: 2. Of those that a mesh axis runs over, the one named last changes fastest.
Arguments:
- child_front: float32 [2, 8192, 8192], P('sib', 'row', 'col'), may hold values from -6 to 6
- child_panel: float32 [2, 8192, 1024], P('sib', ('row', 'col')), may hold values from -0.42 to 0.42
- block_map: int32 [2, 64], replicated, may hold values from 0 to 95, as said below
- parent_front: float32 [12288, 12288], P(('row', 'sib'), 'col'), may hold values from -6 to 6
- pivot_inverse: float32 [512, 512], replicated, may hold values from -0.03 to 0.1, as said below
Outputs:
- parent_out: float32 [12288, 12288], P(('row', 'sib'), 'col')
Inputs may be any that keep to these rules, and one draw needn't show every extreme that they name: `block_map`: each row is strictly increasing. A child block i that lands in parent block g * 6 + k with 0 <= k < 6 satisfies g * 4 - 2 <= i < (g + 1) * 4; the lower end is met for g = 1 in every draw, and the last parent block is always named. `pivot_inverse`: lower triangular with diagonal entries from 0.05 to 0.1.
All inputs are finite; a program needn't handle non-finite values.
Results may differ from a plain program's by a relative error of at most 0.0001.
Values sent between devices are 32-bit elements; how exact they have to be, the bound alone decides.
A program may use at most 64 MiB of HBM per device.

v0:
```python
import jax
import jax.numpy as jnp
from jax import lax
from jax.sharding import Mesh
from jax.sharding import PartitionSpec as P

BLK = 128
CBD = 4
PBD = 6
HB = 2
PANEL = 512
ROW = ("row_0", "row_1")
ROW_COL = ("row_0", "row_1", "col")
ROW_SIB = ("row_0", "row_1", "sib")


def broadcast_by_axis(value, axes, root):
    value = jnp.where(lax.axis_index(axes) == root, value, jnp.zeros_like(value))
    for axis in axes:
        value = lax.psum(value, axis)
    return value


def shifted(value, axis, steps):
    count = lax.axis_size(axis)
    initial, last = (max(0, -steps), min(count, count - steps))
    return lax.ppermute(value, axis, [(source, source + steps) for source in range(initial, last)])


def split_up(value, dim, devices):
    shape = value.shape
    blocks = value.reshape(*shape[:dim], devices, shape[dim] // devices, *shape[dim + 1 :])
    return jnp.moveaxis(blocks, dim, 0)


def summed_on_arrival(value, axis, dim):
    blocks = split_up(value, dim, lax.axis_size(axis))
    arrived = lax.all_to_all(blocks, axis, split_axis=0, concat_axis=0, tiled=True)
    return arrived.sum(axis=0)


def padded_to(lines, devices):
    spare = -len(lines) % devices
    return jnp.pad(lines, [(0, spare)] + [(0, 0)] * (lines.ndim - 1))


def spread(value, axis, root):
    lines = jnp.where(lax.axis_index(axis) == root, value, jnp.zeros_like(value)).reshape(
        -1, *value.shape[1:][-1:]
    )
    padded = padded_to(lines, lax.axis_size(axis))
    own = lax.psum_scatter(padded, axis, scatter_dimension=0, tiled=True)
    return lax.all_gather(own, axis, axis=0, tiled=True)[: len(lines)].reshape(value.shape)


def from_everyone(value, axis):
    devices = lax.axis_size(axis)
    return lax.all_to_all(
        jnp.broadcast_to(value[None], (devices, *value.shape)), axis, 0, 0, tiled=True
    )


def joined_along(blocks, dim):
    shape = list(blocks.shape[1:])
    shape[dim] *= blocks.shape[0]
    return jnp.moveaxis(blocks, 0, dim).reshape(shape)


def collect(value, axis, dim):
    blocks = from_everyone(value, axis)
    return joined_along(blocks, dim)


def choose_blocks(block_row, device, child_span, parent_span, edge_span):
    padded = jnp.concatenate([jnp.full((edge_span,), -1, jnp.int32), block_row])
    window = lax.dynamic_slice_in_dim(padded, device * child_span, child_span + edge_span)
    target = device * parent_span + jnp.arange(parent_span, dtype=jnp.int32)
    return (window[None, :] == target[:, None]).astype(jnp.float32)


def times_inverse(rows_part, pivot_inverse):
    return lax.dot_general(
        rows_part,
        pivot_inverse,
        (((1,), (1,)), ((), ())),
        precision=lax.Precision.HIGHEST,
        preferred_element_type=jnp.float32,
    )


def shards(child_front, child_panel, block_map, parent_front, pivot_inverse):
    front_index = lax.axis_index("sib")
    row_index = lax.axis_index(ROW)
    col_index = lax.axis_index("col")
    child_rows = child_front.shape[1]
    parent_rows = parent_front.shape[0]
    parent_cols = parent_front.shape[1]
    edge_width = HB * BLK
    span_blocks = CBD + HB
    rows_local = lax.all_gather(child_panel, "col", axis=1, tiled=True)[0]
    cols_local = broadcast_by_axis(rows_local, ROW, col_index)
    update = child_front[0] - lax.dot_general(
        rows_local,
        cols_local,
        (((1,), (1,)), ((), ())),
        precision=lax.Precision.HIGHEST,
        preferred_element_type=jnp.float32,
    )
    my_map = lax.dynamic_index_in_dim(block_map, front_index, 0, keepdims=False)
    left_cols = shifted(update[:, -edge_width:], "col", 1)
    col_window = jnp.concatenate([left_cols, update], axis=1).reshape(child_rows, span_blocks, BLK)
    col_pick = choose_blocks(my_map, col_index, CBD, PBD, HB)
    spread_cols = jnp.einsum(
        "rwk,qw->rqk", col_window, col_pick, precision=lax.Precision.HIGHEST
    ).reshape(child_rows, PBD * BLK)
    left_rows = shifted(spread_cols[-edge_width:], ROW, 1)
    row_window = jnp.concatenate([left_rows, spread_cols], axis=0).reshape(
        span_blocks, BLK, PBD * BLK
    )
    row_pick = choose_blocks(my_map, row_index, CBD, PBD, HB)
    spread_both = jnp.einsum(
        "wtc,qw->qtc", row_window, row_pick, precision=lax.Precision.HIGHEST
    ).reshape(PBD * BLK, PBD * BLK)
    summed = summed_on_arrival(spread_both, "sib", 0)
    assembled = parent_front + summed
    local_factor = times_inverse(assembled[:, :PANEL], pivot_inverse)
    factor_rows = spread(local_factor, "col", 0)
    owner_rows = broadcast_by_axis(factor_rows, ROW, col_index)
    col_factor = collect(owner_rows, "sib", 0)
    product = lax.dot_general(
        factor_rows,
        col_factor,
        (((1,), (1,)), ((), ())),
        precision=lax.Precision.HIGHEST,
        preferred_element_type=jnp.float32,
    )
    global_rows = (row_index * 2 + front_index) * parent_rows + jnp.arange(
        parent_rows, dtype=jnp.int32
    )
    global_cols = col_index * parent_cols + jnp.arange(parent_cols, dtype=jnp.int32)
    inside = (global_rows[:, None] >= PANEL) & (global_cols[None, :] >= PANEL)
    trailing = jnp.where(inside, assembled - product, assembled)
    factor_wide = jnp.pad(factor_rows, ((0, 0), (0, parent_cols - PANEL)))
    return jnp.where(global_cols[None, :] < PANEL, factor_wide, trailing)


def solution(mesh):
    split = Mesh(
        mesh.devices.reshape(mesh.shape["sib"], 8, 2, mesh.shape["col"]),
        ("sib", "row_0", "row_1", "col"),
    )
    placed = (P("sib", ROW, "col"), P("sib", ROW_COL, None), P(), P(ROW_SIB, "col"), P())
    return jax.shard_map(
        shards, mesh=split, in_specs=placed, out_specs=P(ROW_SIB, "col"), check_vma=False
    )
```

profile of v0, /device:TPU:1, one launch (start us, length us, event | category | flops | bytes accessed | tf_op | source)
XLA Modules:
  0.0 621.0 jit_solution(6062125449259001521)
XLA Ops:
  6.5 0.0 copy-start
  6.5 0.0 all-gather.2.cloned.1.call-start
  6.5 0.7 all-gather.2.cloned.1.call-update
  7.3 0.0 all-reduce.7.cloned.1.call-start
  7.3 72.9 %all-gather.2.cloned.1.call-done = f32[1,512,1024]{2,1,0:T(8,128)} async-done(((f32[1,32,1024]{2,1,0:T(8,128)}), f32[1,512,1024]{2,1,0:T(8,128)}) %all-gather.2.cloned.1.call-update) | async-done | bytes 2097168 | tf_op jit(solution)/shard_map/all_gather | solution.py:100
  80.2 3.2 bitcast_select_fusion
  83.4 0.0 all-reduce.7.cloned.1.call-update
  83.4 0.0 all-reduce.9.cloned.1.call-start
  83.4 82.9 %all-reduce.7.cloned.1.call-done = f32[512,1024]{1,0:T(8,128)} async-done(((f32[512,1024]{1,0:T(8,128)}), f32[512,1024]{1,0:T(8,128)}) %all-reduce.7.cloned.1.call-update) | async-done | bytes 2097168 | tf_op jit(solution)/shard_map/psum | solution.py:20
  166.4 0.0 copy-start.1
  166.4 0.0 all-reduce.9.cloned.1.call-update
  166.4 0.0 reduce-scatter.2.cloned.1.call-start
  166.4 2.7 copy.8
  169.1 0.0 copy-start.3
  169.1 81.5 %all-reduce.9.cloned.1.call-done = f32[512,1024]{1,0:T(8,128)} async-done(((f32[512,1024]{1,0:T(8,128)}), f32[512,1024]{1,0:T(8,128)}) %all-reduce.9.cloned.1.call-update) | async-done | bytes 2097168 | tf_op jit(solution)/shard_map/psum | solution.py:20
  250.6 0.0 copy-done.1
  250.6 5.4 fusion.8
  256.0 0.0 copy-start.2
  256.0 1.0 copy-done.2
  257.0 4.1 collective-permute-start
  261.1 0.0 copy-done.3
  261.1 0.1 pad_dynamic-slice_fusion.1
  261.2 13.7 %collective-permute-done = f32[512,256]{0,1:T(8,128)S(1)} collective-permute-done((f32[512,256]{0,1:T(8,128)S(1)}, f32[512,256]{0,1:T(8,128)S(1)}, u32[]{:S(2)}, u32[]{:S(2)}) %collective-permute-start) | collective-permute-done | bytes 524320 | tf_op jit(solution)/shard_map/ppermute | solution.py:27
  275.0 1.3 pad_maximum_fusion.1
  276.3 1.8 copy.9
  278.2 2.7 convolution_bitcast_fusion
  280.8 1.0 slice.17
  281.9 2.4 copy.10
  284.3 11.1 %collective-permute-start.1 = (f32[256,768]{0,1:T(8,128)}, f32[256,768]{0,1:T(8,128)}, u32[]{:S(2)}, u32[]{:S(2)}) collective-permute-start(f32[256,768]{0,1:T(8,128)} %bitcast.40), channel_id=1, source_target_pairs={{0,16},{16,32},{32,48},{48,64},{64,80},{80,96},{96,112},{112,128},... | collective-permute-start | bytes 2359304 | tf_op jit(solution)/shard_map/ppermute | solution.py:27
  295.4 1.6 copy.11
  297.0 13.2 %collective-permute-done.1 = f32[256,768]{0,1:T(8,128)} collective-permute-done((f32[256,768]{0,1:T(8,128)}, f32[256,768]{0,1:T(8,128)}, u32[]{:S(2)}, u32[]{:S(2)}) %collective-permute-start.1) | collective-permute-done | bytes 786464 | tf_op jit(solution)/shard_map/ppermute | solution.py:27
  310.2 3.2 pad_maximum_fusion
  313.4 2.0 copy.12
  315.4 2.9 fusion
  318.3 0.8 copy.14
  319.1 7.7 %all_to_all.10 = f32[2,384,768]{2,1,0:T(8,128)S(1)} all-to-all(f32[2,384,768]{2,1,0:T(8,128)S(1)} %bitcast.36), channel_id=1, replica_groups=mesh['sib'=2,'row_0'=8,'row_1'=2,'col'=16] {'sib'}, dimensions={0} | all-to-all | bytes 4718592 | tf_op jit(solution)/shard_map/all_to_all | solution.py:38
  326.8 1.3 reduce_sum.9
  328.0 1.8 add.88
  329.8 0.0 copy-done
  329.8 2.3 convolution_select_fusion
  332.1 0.0 reduce-scatter.2.cloned.1.call-update
  332.2 0.0 all-reduce.11.cloned.1.call-start
  332.2 94.5 %reduce-scatter.2.cloned.1.call-done = f32[24,512]{1,0:T(8,128)} async-done(((f32[384,512]{1,0:T(8,128)}), f32[24,512]{1,0:T(8,128)}) %reduce-scatter.2.cloned.1.call-update) | async-done | bytes 49168 | tf_op jit(solution)/shard_map/reduce_scatter | solution.py:52
  426.7 41.6 %all_gather.7 = f32[384,512]{1,0:T(8,128)S(1)} all-gather(f32[24,512]{1,0:T(8,128)} %reduce-scatter.2.cloned.1.call-done), channel_id=1, replica_groups=mesh['sib'=2,'row_0'=8,'row_1'=2,'col'=16] {'col'}, dimensions={0}, use_global_device_ids=true | all-gather | bytes 835584 | tf_op jit(solution)/shard_map/all_gather | solution.py:53
  468.3 0.9 broadcast_select_fusion
  469.2 0.0 all-reduce.11.cloned.1.call-update
  469.2 0.0 all-reduce.13.cloned.1.call-start
  469.3 78.7 %all-reduce.11.cloned.1.call-done = f32[384,512]{1,0:T(8,128)} async-done(((f32[384,512]{1,0:T(8,128)}), f32[384,512]{1,0:T(8,128)}) %all-reduce.11.cloned.1.call-update) | async-done | bytes 786448 | tf_op jit(solution)/shard_map/psum | solution.py:20
  548.0 0.0 all-reduce.13.cloned.1.call-update
  548.1 56.2 %all-reduce.13.cloned.1.call-done = f32[384,512]{1,0:T(8,128)} async-done(((f32[384,512]{1,0:T(8,128)}), f32[384,512]{1,0:T(8,128)}) %all-reduce.13.cloned.1.call-update) | async-done | bytes 786448 | tf_op jit(solution)/shard_map/psum | solution.py:20
  604.3 1.3 broadcast_in_dim.11
  605.6 5.3 all_to_all.11
  610.9 3.2 fusion.4
  (6 shorter events, 0.1 us)
Async XLA Ops:
  6.5 323.3 %copy-start = (f32[512,512]{1,0:T(8,128)S(1)}, f32[512,512]{1,0:T(8,128)}, u32[]{:S(2)}) copy-start(f32[512,512]{1,0:T(8,128)} %param.9) | copy-start | bytes 3145732
  6.5 73.6 %all-gather.2.cloned.1.call-start = ((), (), s32[]{:S(2)}) async-start(), calls=%async_computation.3 | async-start | bytes 2228224 | tf_op jit(solution)/shard_map/all_gather | solution.py:100
  7.3 159.1 %all-reduce.7.cloned.1.call-start = ((), (), s32[]{:S(2)}) async-start(), calls=%async_computation.4 | async-start | bytes 4194304 | tf_op jit(solution)/shard_map/psum | solution.py:20
  83.4 167.2 %all-reduce.9.cloned.1.call-start = ((), (), s32[]{:S(2)}) async-start(), calls=%async_computation.5 | async-start | bytes 4194304 | tf_op jit(solution)/shard_map/psum | solution.py:20
  166.4 84.2 %copy-start.1 = (f32[1,512,1024]{2,1,0:T(8,128)S(1)}, f32[1,512,1024]{2,1,0:T(8,128)}, u32[]{:S(2)}) copy-start(f32[1,512,1024]{2,1,0:T(8,128)} %all-gather.2.cloned.1.call-done) | copy-start | bytes 6291460
  166.4 260.3 %reduce-scatter.2.cloned.1.call-start = ((), (), s32[]{:S(2)}) async-start(), calls=%async_computation.6 | async-start | bytes 835584 | tf_op jit(solution)/shard_map/reduce_scatter | solution.py:52
  169.1 92.0 %copy-start.3 = (s32[2,64]{1,0:T(2,128)S(1)}, s32[2,64]{1,0:T(2,128)}, u32[]{:S(2)}) copy-start(s32[2,64]{1,0:T(2,128)} %param.7) | copy-start | bytes 1540
  256.0 1.0 copy-start.2
  257.0 17.9 %collective-permute-start = (f32[512,256]{0,1:T(8,128)S(1)}, f32[512,256]{0,1:T(8,128)S(1)}, u32[]{:S(2)}, u32[]{:S(2)}) collective-permute-start(f32[512,256]{0,1:T(8,128)S(1)} %slice.16), channel_id=1, source_target_pairs={{0,1},{1,2},{2,3},{3,4},{4,5},{5,6},{6,7},{7,8},{8,9},{9,10},{10,1... | collective-permute-start | bytes 1572872 | tf_op jit(solution)/shard_map/ppermute | solution.py:27
  284.3 25.9 %collective-permute-start.1 = (f32[256,768]{0,1:T(8,128)}, f32[256,768]{0,1:T(8,128)}, u32[]{:S(2)}, u32[]{:S(2)}) collective-permute-start(f32[256,768]{0,1:T(8,128)} %bitcast.40), channel_id=1, source_target_pairs={{0,16},{16,32},{32,48},{48,64},{64,80},{80,96},{96,112},{112,128},... | collective-permute-start | bytes 2359304 | tf_op jit(solution)/shard_map/ppermute | solution.py:27
  332.2 215.8 %all-reduce.11.cloned.1.call-start = ((), (), s32[]{:S(2)}) async-start(), calls=%async_computation.7 | async-start | bytes 1572864 | tf_op jit(solution)/shard_map/psum | solution.py:20
  469.2 135.1 %all-reduce.13.cloned.1.call-start = ((), (), s32[]{:S(2)}) async-start(), calls=%async_computation.8 | async-start | bytes 1572864 | tf_op jit(solution)/shard_map/psum | solution.py:20
Sparse Core Ops, SparseCore 0:
  10.4 69.7 all-gather.1
  83.5 82.8 all-reduce.6
  169.3 81.2 all-reduce.8
  332.3 94.3 reduce-scatter.1
  469.3 78.6 all-reduce.10
  550.7 53.5 all-reduce.12
where the time goes:
time: 621 us
  waiting for transfers between devices  494 us (80%)
  blocking collectives  54.5 us (9%)
  matrix products  16.5 us (3%)
  starting transfers between devices  15.4 us (2%)
  local copies, waits for them, and re-layouts  14.8 us (2%)
  between operations  13.6 us (2%)
  other arithmetic  11.7 us (2%)
    psum x4, waiting for transfers between devices, broadcast_by_axis(): value = lax.psum(value, axis)  299 us
    reduce_scatter x1, waiting for transfers between devices, spread(): own = lax.psum_scatter(padded, axis, scatter_dimension=0, tiled=True)  94.5 us
    all_gather x1, waiting for transfers between devices, shards(): rows_local = lax.all_gather(child_panel, 'col', axis=1, tiled=True)[0]  72.9 us
    all_gather x1, blocking collectives, spread(): lax.all_gather(own, axis, axis=0, tiled=True)[:len(lines)]  41.6 us
    ppermute x2, waiting for transfers between devices, shifted(): lax.ppermute(value, axis, [(source, source + steps) for source in range(i...  26.9 us
    ppermute x2, starting transfers between devices, shifted(): lax.ppermute(value, axis, [(source, source + steps) for source in range(i...  15.2 us
  transfers between devices with their start and end apart: 8, of which 8 were waited for; matrix products, arithmetic and copies ran while one was open for 1% of the time, Pallas kernels for 0%

commit v1 on v0

--- a/solution.py
+++ b/solution.py
@@ -17,7 +17,8 @@
 def broadcast_by_axis(value, axes, root):
     value = jnp.where(lax.axis_index(axes) == root, value, jnp.zeros_like(value))
     for axis in axes:
-        value = lax.psum(value, axis)
+        earlier = lax.all_gather(value, axis)
+        value = jnp.sum(earlier, 0)
     return value
 
 

time: 621 us -> 689 us (1.11)
  waiting for transfers between devices: 494 us -> 543 us
  other arithmetic: 11.7 us -> 30.7 us
    all_gather x0 -> x4, waiting for transfers between devices: none -> 348 us  [broadcast_by_axis(): earlier = lax.all_gather(value, axis)]
    psum x4 -> x0, waiting for transfers between devices: 299 us -> none  [broadcast_by_axis(): value = lax.psum(value, axis)]
    reduce_sum x0 -> x4, other arithmetic: none -> 19 us  [broadcast_by_axis(): value = jnp.sum(earlier, 0)]
  transfers between devices with their start and end apart: 8 -> 8, of which waited for: 8 -> 8; matrix products, arithmetic and copies ran while one was open for 1% -> 0% of each run, Pallas kernels for 0% -> 0%
where the time goes in v1:
time: 689 us; the launch traced here: 688 us
  waiting for transfers between devices  543 us (79%)
  blocking collectives  54.4 us (8%)
  other arithmetic  30.7 us (4%)
  matrix products  16.5 us (2%)
  starting transfers between devices  15.4 us (2%)
  local copies, waits for them, and re-layouts  14.6 us (2%)
  between operations  13.6 us (2%)
    all_gather x4, waiting for transfers between devices, broadcast_by_axis(): earlier = lax.all_gather(value, axis)  348 us
    reduce_scatter x1, waiting for transfers between devices, spread(): own = lax.psum_scatter(padded, axis, scatter_dimension=0, tiled=True)  94.6 us
    all_gather x1, waiting for transfers between devices, shards(): rows_local = lax.all_gather(child_panel, 'col', axis=1, tiled=True)[0]  72.9 us
    all_gather x1, blocking collectives, spread(): lax.all_gather(own, axis, axis=0, tiled=True)[:len(lines)]  41.5 us
    ppermute x2, waiting for transfers between devices, shifted(): lax.ppermute(value, axis, [(source, source + steps) for source in range(i...  26.9 us
    reduce_sum x4, other arithmetic, broadcast_by_axis(): value = jnp.sum(earlier, 0)  19 us
    ppermute x2, starting transfers between devices, shifted(): lax.ppermute(value, axis, [(source, source + steps) for source in range(i...  15.2 us
  transfers between devices with their start and end apart: 8, of which 8 were waited for; matrix products, arithmetic and copies ran while one was open for 0% of the time, Pallas kernels for 0%

profile of v1, /device:TPU:1, one launch (start us, length us, event | category | flops | bytes accessed | tf_op | source)
XLA Modules:
  0.0 688.1 jit_solution(6151833570485412134)
XLA Ops:
  6.5 0.0 copy-start
  6.5 0.0 all-gather.9.cloned.1.call-start
  6.5 0.7 all-gather.9.cloned.1.call-update
  7.3 0.0 all-gather.11.cloned.1.call-start
  7.3 72.9 %all-gather.9.cloned.1.call-done = f32[1,512,1024]{2,1,0:T(8,128)} async-done(((f32[1,32,1024]{2,1,0:T(8,128)}), f32[1,512,1024]{2,1,0:T(8,128)}) %all-gather.9.cloned.1.call-update) | async-done | bytes 2097168 | tf_op jit(solution)/shard_map/all_gather | solution.py:101
  80.2 3.2 broadcast_select_fusion
  83.3 0.0 all-gather.11.cloned.1.call-update
  83.4 0.0 all-gather.13.cloned.1.call-start
  83.4 173.4 %all-gather.11.cloned.1.call-done = f32[8,512,1024]{2,1,0:T(8,128)} async-done(((f32[1,512,1024]{2,1,0:T(8,128)}), f32[8,512,1024]{2,1,0:T(8,128)}) %all-gather.11.cloned.1.call-update) | async-done | bytes 16777232 | tf_op jit(solution)/shard_map/all_gather | solution.py:20
  256.8 9.3 %reduce_sum.45 = f32[512,1024]{1,0:T(8,128)} reduce(f32[8,512,1024]{2,1,0:T(8,128)} %all-gather.11.cloned.1.call-done, f32[]{:T(128)} %constant.45.clone.1), dimensions={0}, to_apply=%region_0.1 | reduce | flops 3670016 | bytes 18874372 | tf_op jit(solution)/shard_map/reduce_sum | solution.py:21
  266.1 0.0 copy-start.2
  266.1 0.0 all-gather.13.cloned.1.call-update
  266.1 0.0 reduce-scatter.2.cloned.1.call-start
  266.1 1.1 copy-done.2
  267.3 1.3 copy.22
  268.6 60.4 %all-gather.13.cloned.1.call-done = f32[1024,1024]{1,0:T(8,128)} async-done(((f32[512,1024]{1,0:T(8,128)}), f32[1024,1024]{1,0:T(8,128)}) %all-gather.13.cloned.1.call-update) | async-done | bytes 4194320 | tf_op jit(solution)/shard_map/all_gather | solution.py:20
  329.0 2.8 reduce_sum.46
  331.8 0.0 copy-start.3
  331.8 5.4 fusion.8
  337.2 0.0 copy-start.1
  337.2 1.0 copy-done.1
  338.2 4.1 collective-permute-start
  342.3 0.0 copy-done.3
  342.3 0.1 pad_dynamic-slice_fusion.1
  342.4 13.7 %collective-permute-done = f32[512,256]{0,1:T(8,128)S(1)} collective-permute-done((f32[512,256]{0,1:T(8,128)S(1)}, f32[512,256]{0,1:T(8,128)S(1)}, u32[]{:S(2)}, u32[]{:S(2)}) %collective-permute-start) | collective-permute-done | bytes 524320 | tf_op jit(solution)/shard_map/ppermute | solution.py:28
  356.2 1.3 pad_maximum_fusion.1
  357.5 1.8 copy.23
  359.4 2.7 convolution_bitcast_fusion
  362.0 1.0 slice.17
  363.1 2.4 copy.24
  365.5 11.1 %collective-permute-start.1 = (f32[256,768]{0,1:T(8,128)}, f32[256,768]{0,1:T(8,128)}, u32[]{:S(2)}, u32[]{:S(2)}) collective-permute-start(f32[256,768]{0,1:T(8,128)} %bitcast.45), channel_id=1, source_target_pairs={{0,16},{16,32},{32,48},{48,64},{64,80},{80,96},{96,112},{112,128},... | collective-permute-start | bytes 2359304 | tf_op jit(solution)/shard_map/ppermute | solution.py:28
  376.6 1.6 copy.25
  378.2 13.2 %collective-permute-done.1 = f32[256,768]{0,1:T(8,128)} collective-permute-done((f32[256,768]{0,1:T(8,128)}, f32[256,768]{0,1:T(8,128)}, u32[]{:S(2)}, u32[]{:S(2)}) %collective-permute-start.1) | collective-permute-done | bytes 786464 | tf_op jit(solution)/shard_map/ppermute | solution.py:28
  391.4 3.2 pad_maximum_fusion
  394.6 2.0 copy.26
  396.6 2.9 fusion
  399.5 0.8 copy.28
  400.3 7.6 %all_to_all.10 = f32[2,384,768]{2,1,0:T(8,128)S(1)} all-to-all(f32[2,384,768]{2,1,0:T(8,128)S(1)} %bitcast.38), channel_id=1, replica_groups=mesh['sib'=2,'row_0'=8,'row_1'=2,'col'=16] {'sib'}, dimensions={0} | all-to-all | bytes 4718592 | tf_op jit(solution)/shard_map/all_to_all | solution.py:39
  407.9 1.3 reduce_sum.47
  409.2 1.8 add.80
  410.9 0.0 copy-done
  410.9 2.3 convolution_select_fusion
  413.3 0.0 reduce-scatter.2.cloned.1.call-update
  413.3 0.0 all-gather.15.cloned.1.call-start
  413.3 94.6 %reduce-scatter.2.cloned.1.call-done = f32[24,512]{1,0:T(8,128)} async-done(((f32[384,512]{1,0:T(8,128)}), f32[24,512]{1,0:T(8,128)}) %reduce-scatter.2.cloned.1.call-update) | async-done | bytes 49168 | tf_op jit(solution)/shard_map/reduce_scatter | solution.py:53
  507.9 41.5 %all_gather.32 = f32[384,512]{1,0:T(8,128)S(1)} all-gather(f32[24,512]{1,0:T(8,128)} %reduce-scatter.2.cloned.1.call-done), channel_id=1, replica_groups=mesh['sib'=2,'row_0'=8,'row_1'=2,'col'=16] {'col'}, dimensions={0}, use_global_device_ids=true | all-gather | bytes 835584 | tf_op jit(solution)/shard_map/all_gather | solution.py:54
  549.4 0.9 broadcast_select_fusion.1
  550.4 0.0 all-gather.15.cloned.1.call-update
  550.4 0.0 all-gather.17.cloned.1.call-start
  550.5 80.7 %all-gather.15.cloned.1.call-done = f32[3072,512]{1,0:T(8,128)} async-done(((f32[384,512]{1,0:T(8,128)}), f32[3072,512]{1,0:T(8,128)}) %all-gather.15.cloned.1.call-update) | async-done | bytes 6291472 | tf_op jit(solution)/shard_map/all_gather | solution.py:20
  631.1 4.5 reduce_sum.48
  635.6 0.0 all-gather.17.cloned.1.call-update
  635.7 33.3 %all-gather.17.cloned.1.call-done = f32[768,512]{1,0:T(8,128)} async-done(((f32[384,512]{1,0:T(8,128)}), f32[768,512]{1,0:T(8,128)}) %all-gather.17.cloned.1.call-update) | async-done | bytes 1572880 | tf_op jit(solution)/shard_map/all_gather | solution.py:20
  668.9 2.5 reduce_sum.49
  671.4 1.3 broadcast_in_dim.11
  672.8 5.3 all_to_all.11
  678.1 3.2 fusion.4
  (6 shorter events, 0.1 us)
Async XLA Ops:
  6.5 404.4 %copy-start = (f32[512,512]{1,0:T(8,128)S(1)}, f32[512,512]{1,0:T(8,128)}, u32[]{:S(2)}) copy-start(f32[512,512]{1,0:T(8,128)} %param.9) | copy-start | bytes 3145732
  6.5 73.6 %all-gather.9.cloned.1.call-start = ((), (), s32[]{:S(2)}) async-start(), calls=%async_computation.3 | async-start | bytes 2228224 | tf_op jit(solution)/shard_map/all_gather | solution.py:101
  7.3 249.5 %all-gather.11.cloned.1.call-start = ((), (), s32[]{:S(2)}) async-start(), calls=%async_computation.4 | async-start | bytes 18874368 | tf_op jit(solution)/shard_map/all_gather | solution.py:20
  83.4 245.6 %all-gather.13.cloned.1.call-start = ((), (), s32[]{:S(2)}) async-start(), calls=%async_computation.6 | async-start | bytes 6291456 | tf_op jit(solution)/shard_map/all_gather | solution.py:20
  266.1 1.2 copy-start.2
  266.1 241.8 %reduce-scatter.2.cloned.1.call-start = ((), (), s32[]{:S(2)}) async-start(), calls=%async_computation.5 | async-start | bytes 835584 | tf_op jit(solution)/shard_map/reduce_scatter | solution.py:53
  331.8 10.5 %copy-start.3 = (s32[2,64]{1,0:T(2,128)S(1)}, s32[2,64]{1,0:T(2,128)}, u32[]{:S(2)}) copy-start(s32[2,64]{1,0:T(2,128)} %param.7) | copy-start | bytes 1540
  337.2 1.0 copy-start.1
  338.2 17.9 %collective-permute-start = (f32[512,256]{0,1:T(8,128)S(1)}, f32[512,256]{0,1:T(8,128)S(1)}, u32[]{:S(2)}, u32[]{:S(2)}) collective-permute-start(f32[512,256]{0,1:T(8,128)S(1)} %slice.16), channel_id=1, source_target_pairs={{0,1},{1,2},{2,3},{3,4},{4,5},{5,6},{6,7},{7,8},{8,9},{9,10},{10,1... | collective-permute-start | bytes 1572872 | tf_op jit(solution)/shard_map/ppermute | solution.py:28
  365.5 25.9 %collective-permute-start.1 = (f32[256,768]{0,1:T(8,128)}, f32[256,768]{0,1:T(8,128)}, u32[]{:S(2)}, u32[]{:S(2)}) collective-permute-start(f32[256,768]{0,1:T(8,128)} %bitcast.45), channel_id=1, source_target_pairs={{0,16},{16,32},{32,48},{48,64},{64,80},{80,96},{96,112},{112,128},... | collective-permute-start | bytes 2359304 | tf_op jit(solution)/shard_map/ppermute | solution.py:28
  413.3 217.8 %all-gather.15.cloned.1.call-start = ((), (), s32[]{:S(2)}) async-start(), calls=%async_computation.7 | async-start | bytes 7077888 | tf_op jit(solution)/shard_map/all_gather | solution.py:20
  550.4 118.5 %all-gather.17.cloned.1.call-start = ((), (), s32[]{:S(2)}) async-start(), calls=%async_computation.8 | async-start | bytes 2359296 | tf_op jit(solution)/shard_map/all_gather | solution.py:20
Sparse Core Ops, SparseCore 0:
  10.4 69.7 all-gather.8
  83.5 173.2 all-gather.10
  266.2 62.7 all-gather.12
  413.4 94.4 reduce-scatter.1
  550.5 80.5 all-gather.14
  635.7 33.1 all-gather.16
